TPU v7x, 32 devices: a whole 2x2x4 slice. The times are simulated.
32 devices in a mesh: gx: 8 (over z, x), gy: 4 (over y, core).
Axes of the slice: x: 2, y: 2, z: 4, core: 2. Of those that a mesh axis runs over, the one named last changes fastest.
Arguments:
- field: float32 [64, 32, 192], P('gx', 'gy'), may hold values from -6 to 6
- target: float32 [64, 32, 192], P('gx', 'gy'), may hold values from -6 to 6
- embed_weight: float32 [192, 256], replicated, may hold values from -0.4375 to 0.4375
- norm_gain: float32 [256], replicated, may hold values from 0.5 to 1.5
- attend_weight: float32 [256, 768], replicated, may hold values from -0.375 to 0.375
- output_weight: float32 [256, 256], replicated, may hold values from -0.375 to 0.375
- second_gain: float32 [256], replicated, may hold values from 0.5 to 1.5
- expand_weight: float32 [256, 512], replicated, may hold values from -0.375 to 0.375
- reduce_weight: float32 [512, 256], replicated, may hold values from -0.25 to 0.25
- decode_weight: float32 [256, 192], replicated, may hold values from -0.375 to 0.375
Outputs:
- loss: float32 [], replicated
- field_gradient: float32 [64, 32, 192], P('gx', 'gy')
- embed_gradient: float32 [192, 256], replicated
- norm_gradient: float32 [256], replicated
- attend_gradient: float32 [256, 768], replicated
- output_gradient: float32 [256, 256], replicated
- second_gradient: float32 [256], replicated
- expand_gradient: float32 [256, 512], replicated
- reduce_gradient: float32 [512, 256], replicated
- decode_gradient: float32 [256, 192], replicated
All inputs are finite; a program needn't handle non-finite values.
Results may differ from a plain program's by a relative error of at most 0.0001.
Values sent between devices are 32-bit elements; how exact they have to be, the bound alone decides.
A program may use at most 128 MiB of HBM per device.

v0:
```python
import functools

import jax
import jax.numpy as jnp
import numpy as np
from jax import lax
from jax.experimental import pallas as pl
from jax.experimental.pallas import tpu as pltpu
from jax.sharding import PartitionSpec as P

PATCH = 4
HEADS = 8
STEPS = 2

EPSILON = 1e-06
TIME_STEP = 0.1
VISCOSITY = 0.5
LANES = 128
MESH = pl.DeviceIdType.MESH
VMEM_LIMIT = 56 * 1024 * 1024
F32 = jnp.float32


def dot(left, right, dims):
    lh = left.astype(jnp.bfloat16)
    rh = right.astype(jnp.bfloat16)
    ll = (left - lh.astype(F32)).astype(jnp.bfloat16)
    rl = (right - rh.astype(F32)).astype(jnp.bfloat16)
    one = lambda a, b: lax.dot_general(a, b, (dims, ((), ())), preferred_element_type=F32)
    return one(lh, rh) + (one(lh, rl) + one(ll, rh))


def nn(a, b):
    return dot(a, b, ((1,), (0,)))


def nt(a, b):
    return dot(a, b, ((1,), (1,)))


def tn(a, b):
    return dot(a, b, ((0,), (0,)))


class Shape:
    def __init__(self, field_shape, width, hidden):
        wide, tall, depth = field_shape
        self.ax, self.ay, self.up = wide // PATCH, tall // PATCH, depth // 3 // PATCH
        self.ex, self.ey = self.ax + 2, self.ay + 2
        self.inner = self.ax * self.ay * self.up
        self.ext = self.ex * self.ey * self.up
        self.cube = PATCH**3
        self.feat = 4 * self.cube
        self.width, self.hidden = width, hidden

    def row(self, x, y):
        return (x * self.ey + y) * self.up

    def view(self, dx, dy):
        return [(self.row(x + 1 + dx, 1 + dy), self.ay * self.up) for x in range(self.ax)]

    def copies(self):
        out = []
        for dx in (-1, 0, 1):
            for dy in (-1, 0, 1):
                if dx == 0 and dy == 0:
                    continue
                xs = {1: [(self.ax - 1, 0)], -1: [(0, self.ex - 1)], 0: [(x, x + 1) for x in range(self.ax)]}[dx]
                ys = {1: (self.ay - 1, 0, 1), -1: (0, self.ey - 1, 1), 0: (0, 1, self.ay)}[dy]
                for src, dst in xs:
                    out.append(
                        (dx, dy, (src * self.ay + ys[0]) * self.up, self.row(dst, ys[1]), ys[2] * self.up)
                    )
        return out


def take(value, spans):
    return jnp.concatenate([value[s : s + n] for s, n in spans], axis=0)


def lroll(value, shift):
    return pltpu.roll(value, shift % value.shape[1], 1)


def iota(shape, dim):
    return lax.broadcasted_iota(jnp.int32, shape, dim)


def stencil_parts(sh, ext):
    shape = (sh.inner, sh.feat)
    lane = iota(shape, 1)
    px, py, pz = (lane // (PATCH * PATCH)) % PATCH, (lane // PATCH) % PATCH, lane % PATCH
    comp = lane // sh.cube
    level = iota(shape, 0) % sh.up
    u = take(ext, sh.view(0, 0))
    last = PATCH - 1

    def plus(here, there, pos, stride):
        return jnp.where(pos < last, lroll(here, -stride), lroll(there, last * stride))

    def minus(here, there, pos, stride):
        return jnp.where(pos > 0, lroll(here, stride), lroll(there, -last * stride))

    above = jnp.where(level == sh.up - 1, 0.0, pltpu.roll(u, sh.inner - 1, 0))
    below = jnp.where(level == 0, 0.0, pltpu.roll(u, 1, 0))
    sx, sy = PATCH * PATCH, PATCH
    east = plus(u, take(ext, sh.view(1, 0)), px, sx)
    west = minus(u, take(ext, sh.view(-1, 0)), px, sx)
    north = plus(u, take(ext, sh.view(0, 1)), py, sy)
    south = minus(u, take(ext, sh.view(0, -1)), py, sy)
    upper = plus(u, above, pz, 1)
    lower = minus(u, below, pz, 1)
    r1, r2, r3 = lroll(u, sh.cube), lroll(u, 2 * sh.cube), lroll(u, 3 * sh.cube)
    first, second = comp == 0, comp == 1
    vx = jnp.where(first, u, jnp.where(second, r1, r2))
    vy = jnp.where(first, r3, jnp.where(second, u, r1))
    vz = jnp.where(first, r2, jnp.where(second, r3, u))
    return u, (east, west, north, south, upper, lower), (vx, vy, vz), (px, py, pz, comp, level)


def stencil(sh, ext, closed):
    u, (east, west, north, south, upper, lower), (vx, vy, vz), _ = stencil_parts(sh, ext)
    laplace = east + west + north + south + upper + lower - 6.0 * u
    carried = 0.5 * (vx * (east - west) + vy * (north - south) + vz * (upper - lower))
    return u + TIME_STEP * (VISCOSITY * laplace - carried + closed)


def stencil_back(sh, ext, cot, out_ref):
    u, (east, west, north, south, upper, lower), (vx, vy, vz), where = stencil_parts(sh, ext)
    px, py, pz, comp, level = where
    g = TIME_STEP * cot
    total = cot - (6.0 * VISCOSITY) * g

    def summed(value):
        return (
            value
            + lroll(value, sh.cube)
            + lroll(value, 2 * sh.cube)
            + lroll(value, 3 * sh.cube)
        )

    fx = summed(-0.5 * g * (east - west))
    fy = summed(-0.5 * g * (north - south))
    fz = summed(-0.5 * g * (upper - lower))
    total += jnp.where(comp == 0, fx, jnp.where(comp == 1, fy, jnp.where(comp == 2, fz, 0.0)))
    last = PATCH - 1

    def sides(pos, stride, speed):
        high = g * (VISCOSITY - 0.5 * speed)
        low = g * (VISCOSITY + 0.5 * speed)
        here = lroll(jnp.where(pos < last, high, 0.0), stride) + lroll(jnp.where(pos > 0, low, 0.0), -stride)
        after = lroll(jnp.where(pos == last, high, 0.0), -last * stride)
        before = lroll(jnp.where(pos == 0, low, 0.0), last * stride)
        return here, after, before

    here, east_back, west_back = sides(px, PATCH * PATCH, vx)
    total += here
    here, north_back, south_back = sides(py, PATCH, vy)
    total += here
    here, above_back, below_back = sides(pz, 1, vz)
    total += here
    total += jnp.where(level == 0, 0.0, pltpu.roll(above_back, 1, 0))
    total += jnp.where(level == sh.up - 1, 0.0, pltpu.roll(below_back, sh.inner - 1, 0))
    for value, shift in (
        (total, (0, 0)),
        (east_back, (1, 0)),
        (west_back, (-1, 0)),
        (north_back, (0, 1)),
        (south_back, (0, -1)),
    ):
        at = 0
        for s, n in sh.view(*shift):
            out_ref[s : s + n, :] += value[at : at + n]
            at += n


def head_split(sh, value):
    head = iota(value.shape, 1) // (sh.width // HEADS)
    return jnp.concatenate([jnp.where(head == h, value, 0.0) for h in range(HEADS)], axis=0)


def head_join(sh, value):
    head = iota((sh.inner, sh.width), 1) // (sh.width // HEADS)
    total = jnp.zeros((sh.inner, sh.width), F32)
    for h in range(HEADS):
        total = jnp.where(head == h, value[h * sh.inner : (h + 1) * sh.inner], total)
    return total


def inverse_rms(value):
    return lax.rsqrt(jnp.mean(value * value, axis=-1, keepdims=True) + EPSILON)


def forward(sh, ext, w):
    we, g1, wa, wo, g2, wx, wr, wd = w
    d = sh.width
    tokens = nn(ext, we[...])
    normed = tokens * inverse_rms(tokens) * g1[...]
    queries = nn(take(normed, sh.view(0, 0)), wa[:, :d])
    mixed = nn(normed, wa[:, d:])
    keys, values = mixed[:, :d], mixed[:, d:]
    shape = (HEADS * sh.inner, sh.ext)
    qcol = (iota(shape, 0) % sh.inner) // sh.up
    kcol = iota(shape, 1) // sh.up
    dx = kcol // sh.ey - qcol // sh.ay
    dy = kcol % sh.ey - qcol % sh.ay
    seen = (dx >= 0) & (dx <= 2) & (dy >= 0) & (dy <= 2)
    scores = nt(head_split(sh, queries), keys) * ((d // HEADS) ** -0.5)
    weights = jnp.exp(jnp.where(seen, scores, -1e30))
    weights = weights / jnp.sum(weights, axis=-1, keepdims=True)
    attended = head_join(sh, nn(weights, values))
    mid = take(tokens, sh.view(0, 0)) + nn(attended, wo[...])
    pre = nn(mid * inverse_rms(mid) * g2[...], wx[...])
    late = mid + nn(pre / (1.0 + jnp.exp(-pre)), wr[...])
    return nn(late, wd[...]), (tokens, queries, keys, values, weights, attended, mid, pre, late)


def backward(sh, ext, w, saved, cot, back_ref, emit):
    we, g1, wa, wo, g2, wx, wr, wd = w
    d = sh.width
    tokens, queries, keys, values, weights, attended, mid, pre, late = saved
    dclosed = TIME_STEP * cot
    emit("decode", tn(late, dclosed))
    dlate = nt(dclosed, wd[...])
    sig = 1.0 / (1.0 + jnp.exp(-pre))
    emit("reduce", tn(pre * sig, dlate))
    dpre = nt(dlate, wr[...]) * (sig * (1.0 + pre * (1.0 - sig)))
    r2 = inverse_rms(mid)
    unit = mid * r2
    emit("expand", tn(unit * g2[...], dpre))
    dn = nt(dpre, wx[...])
    emit("second", jnp.sum(dn * unit, axis=0, keepdims=True))
    y = dn * g2[...]
    dmid = dlate + r2 * (y - unit * jnp.mean(y * unit, axis=-1, keepdims=True))
    emit("output", tn(attended, dmid))
    dsplit = head_split(sh, nt(dmid, wo[...]))
    dweights = nt(dsplit, values)
    dvalues = tn(weights, dsplit)
    dscores = weights * (dweights - jnp.sum(dweights * weights, axis=-1, keepdims=True))
    dscores = dscores * ((d // HEADS) ** -0.5)
    dqueries = head_join(sh, nn(dscores, keys))
    dkeys = tn(dscores, head_split(sh, queries))
    r1 = inverse_rms(tokens)
    unit = tokens * r1
    normed = unit * g1[...]
    emit("query", tn(take(normed, sh.view(0, 0)), dqueries))
    emit("key", tn(normed, dkeys))
    emit("value", tn(normed, dvalues))
    dn = nt(dkeys, wa[:, d : 2 * d]) + nt(dvalues, wa[:, 2 * d :])
    dinner = nt(dqueries, wa[:, :d])
    back_ref[...] = dn
    at = 0
    for s, n in sh.view(0, 0):
        back_ref[s : s + n, :] += dinner[at : at + n]
        at += n
    dn = back_ref[...]
    emit("norm", jnp.sum(dn * unit, axis=0, keepdims=True))
    y = dn * g1[...]
    back_ref[...] = r1 * (y - unit * jnp.mean(y * unit, axis=-1, keepdims=True))
    at = 0
    for s, n in sh.view(0, 0):
        back_ref[s : s + n, :] += dmid[at : at + n]
        at += n
    dtokens = back_ref[...]
    emit("embed", tn(ext, dtokens))
    back_ref[...] = nt(dtokens, we[...])
    stencil_back(sh, ext, cot, back_ref)


class Packing:
    def __init__(self, sh, devices):
        d = sh.width
        sizes = [
            ("reduce", sh.hidden),
            ("expand", d * (sh.hidden // d)),
            ("decode", d),
            ("output", d),
            ("query", d),
            ("key", d),
            ("value", d),
            ("embed", sh.feat - sh.cube),
            ("small", 8),
        ]
        self.at, row = {}, 0
        for name, n in sizes:
            self.at[name] = (row, n)
            row += n
        unit = 8 * devices
        self.rows = -(-row // unit) * unit
        self.used = row
        self.unit = unit


SMALL = {"norm": 0, "second": 1, "misfit": 2, "energy": 3}


def make_emit(sh, pk, out_ref, prior):
    def emit(name, value):
        if name in SMALL:
            r = pk.at["small"][0] + SMALL[name]
            value = value if prior is None else value + prior[r : r + 1, :]
            out_ref[r : r + 1, :] = value
            return
        row, n = pk.at[name]
        if name == "embed":
            value = value[:n]
        pieces = [value]
        if name == "expand":
            pieces = [value[:, k : k + sh.width] for k in range(0, sh.hidden, sh.width)]
        for piece in pieces:
            m = piece.shape[0]
            add = piece if prior is None else piece + prior[row : row + m, :]
            out_ref[row : row + m, :] = add
            row += m

    return emit


def first_kernel(sh, *refs):
    ext, w, (new, *saved) = refs[0], refs[1:9], refs[9:]
    e = ext[...]
    closed, kept = forward(sh, e, w)
    new[...] = stencil(sh, e, closed)
    for ref, value in zip(saved, kept):
        ref[...] = value


def middle_kernel(sh, pk, *refs):
    ext, target, w, (back, packed) = refs[0], refs[1], refs[2:10], refs[10:12]
    packed[pk.at["small"][0] :, :] = jnp.zeros((pk.rows - pk.at["small"][0], sh.width), F32)
    emit = make_emit(sh, pk, packed, None)
    e = ext[...]
    closed, kept = forward(sh, e, w)
    goal = target[...]
    residue = stencil(sh, e, closed) - goal
    emit("misfit", jnp.sum(residue * residue, axis=0, keepdims=True))
    emit("energy", jnp.sum(goal * goal, axis=0, keepdims=True))
    backward(sh, e, w, kept, 2.0 * residue, back, emit)


def last_kernel(sh, pk, *refs):
    ext, cot, w, saved, prior, (back, packed) = refs[0], refs[1], refs[2:10], refs[10:19], refs[19], refs[20:22]
    packed[pk.at["small"][0] :, :] = prior[pk.at["small"][0] :, :]
    emit = make_emit(sh, pk, packed, prior)
    kept = tuple(ref[...] for ref in saved)
    backward(sh, ext[...], w, kept, cot[...], back, emit)


def neighbour(counts, dx, dy):
    nx, ny = counts
    return (
        lax.rem(lax.axis_index("gx") + (dx + nx), nx),
        lax.rem(lax.axis_index("gy") + (dy + ny), ny),
    )


def greet(devices):
    barrier = pltpu.get_barrier_semaphore()
    for device in devices:
        pl.semaphore_signal(barrier, inc=1, device_id=device, device_id_type=MESH)
    pl.semaphore_wait(barrier, len(devices))


AROUND = [(dx, dy) for dx in (-1, 0, 1) for dy in (-1, 0, 1) if (dx, dy) != (0, 0)]


def spread_kernel(sh, counts, u, ext, send, recv):
    greet([neighbour(counts, dx, dy) for dx, dy in AROUND])
    started = []
    for i, (dx, dy, src, dst, n) in enumerate(sh.copies()):
        copy = pltpu.make_async_remote_copy(
            src_ref=u.at[pl.ds(src, n)],
            dst_ref=ext.at[pl.ds(dst, n)],
            send_sem=send.at[i],
            recv_sem=recv.at[i],
            device_id=neighbour(counts, dx, dy),
            device_id_type=MESH,
        )
        copy.start()
        started.append(copy)
    at = 0
    for s, n in sh.view(0, 0):
        ext[s : s + n, :] = u[at : at + n, :]
        at += n
    for copy in started:
        copy.wait()


def gather_kernel(sh, counts, back, out, slots, send, recv):
    greet([neighbour(counts, dx, dy) for dx, dy in AROUND])
    started = []
    place = 0
    for i, (dx, dy, dst, src, n) in enumerate(sh.copies()):
        copy = pltpu.make_async_remote_copy(
            src_ref=back.at[pl.ds(src, n)],
            dst_ref=slots.at[pl.ds(place, n)],
            send_sem=send.at[i],
            recv_sem=recv.at[i],
            device_id=neighbour(counts, -dx, -dy),
            device_id_type=MESH,
        )
        copy.start()
        started.append((copy, dst, place, n))
        place += n
    at = 0
    for s, n in sh.view(0, 0):
        out[at : at + n, :] = back[s : s + n, :]
        at += n
    for copy, dst, place, n in started:
        copy.wait()
        out[dst : dst + n, :] += slots[place : place + n, :]


def exchange_orders(counts):
    nx, ny = counts
    bits = lambda n: [1 << k for k in range(n.bit_length() - 1)]
    ys = [("gy", s) for s in bits(ny)]
    xs = [("gx", s) for s in bits(nx)]
    head, y, x, z = ys[:1], ys[1:], xs[:1], xs[1:]
    return [head + y + x + z, head + x + z + y, head + z + y + x]


def partner(axis, s):
    gx, gy = lax.axis_index("gx"), lax.axis_index("gy")
    index = gx if axis == "gx" else gy
    bit = lax.rem(index // s, 2)
    other = index + s - 2 * s * bit
    return bit, ((other, gy) if axis == "gx" else (gx, other))


def reduce_kernel(counts, parts, packed, out, acc, slots, send, recv):
    orders = exchange_orders(counts)
    greet([partner(*step)[1] for step in orders[0]])
    steps = len(orders[0])
    where = []
    base = 0
    for start, rows in parts:
        where.append([start, rows, base])
        base += rows
    source = packed
    history = [[] for _ in parts]
    for k in range(steps):
        flight = []
        for p, (start, rows, base) in enumerate(where):
            bit, device = partner(*orders[p][k])
            half = rows // 2
            keep = pl.multiple_of(start + bit * half, 8)
            give = pl.multiple_of(start + half - bit * half, 8)
            copy = pltpu.make_async_remote_copy(
                src_ref=source.at[pl.ds(give, half)],
                dst_ref=slots.at[pl.ds(base, half)],
                send_sem=send.at[p, k],
                recv_sem=recv.at[p, k],
                device_id=device,
                device_id_type=MESH,
            )
            copy.start()
            flight.append((copy, keep, half, base))
            history[p].append((keep, half, device))
        for p, (copy, keep, half, base) in enumerate(flight):
            copy.wait()
            target = acc if k < steps - 1 else out
            target[pl.ds(keep, half), :] = source[pl.ds(keep, half), :] + slots[pl.ds(base, half), :]
            where[p] = [keep, half, base + half]
        source = acc
    for k in reversed(range(steps)):
        flight = []
        for p in range(len(parts)):
            keep, half, device = history[p][k]
            copy = pltpu.make_async_remote_copy(
                src_ref=out.at[pl.ds(keep, half)],
                dst_ref=out.at[pl.ds(keep, half)],
                send_sem=send.at[p, steps + k],
                recv_sem=recv.at[p, steps + k],
                device_id=device,
                device_id_type=MESH,
            )
            copy.start()
            flight.append(copy)
        for copy in flight:
            copy.wait()


def finish_kernel(sh, pk, entries, packed, cot, loss, field, embed, norm, attend, output, second, expand, reduce, decode):
    small = pk.at["small"][0]
    energy = jnp.sum(packed[small + SMALL["energy"] : small + SMALL["energy"] + 1, :], axis=1, keepdims=True)
    misfit = jnp.sum(packed[small + SMALL["misfit"] : small + SMALL["misfit"] + 1, :], axis=1, keepdims=True)
    scale = entries / energy
    loss[...] = misfit / energy
    field[...] = scale * cot[...]
    norm[...] = scale * packed[small : small + 1, :]
    second[...] = scale * packed[small + 1 : small + 2, :]

    def piece(name):
        row, n = pk.at[name]
        return scale * packed[row : row + n, :]

    embed[...] = piece("embed")
    output[...] = piece("output")
    reduce[...] = piece("reduce")
    decode[...] = piece("decode")[:, : decode.shape[1]]
    d = sh.width
    for k, name in enumerate(("query", "key", "value")):
        attend[:, k * d : (k + 1) * d] = piece(name)
    row = pk.at["expand"][0]
    for k in range(sh.hidden // d):
        expand[:, k * d : (k + 1) * d] = scale * packed[row + k * d : row + (k + 1) * d, :]


def call(kernel, outs, args, scratch=(), collective=None):
    vm = pl.BlockSpec(memory_space=pltpu.VMEM)
    extra = {} if collective is None else dict(collective_id=collective, has_side_effects=True)
    return pl.pallas_call(
        kernel,
        out_shape=[jax.ShapeDtypeStruct(s, F32) for s in outs],
        in_specs=[vm] * len(args),
        out_specs=[vm] * len(outs),
        scratch_shapes=list(scratch),
        compiler_params=pltpu.CompilerParams(vmem_limit_bytes=VMEM_LIMIT, **extra),
    )(*args)


def to_tokens(sh, block):
    x = block.reshape(sh.ax, PATCH, sh.ay, PATCH, 3, sh.up, PATCH).transpose(0, 2, 5, 4, 1, 3, 6)
    return jnp.pad(x.reshape(sh.inner, 3 * sh.cube), ((0, 0), (0, sh.cube)))


def from_tokens(sh, tokens, shape):
    x = tokens[:, : 3 * sh.cube].reshape(sh.ax, sh.ay, sh.up, 3, PATCH, PATCH, PATCH)
    return x.transpose(0, 4, 1, 5, 3, 2, 6).reshape(shape)


def shards(counts, field, target, embed_weight, norm_gain, attend_weight, output_weight, second_gain, expand_weight, reduce_weight, decode_weight):
    width, hidden = expand_weight.shape
    sh = Shape(field.shape, width, hidden)
    devices = counts[0] * counts[1]
    pk = Packing(sh, devices)
    blocks = pk.rows // pk.unit
    cuts = [blocks * k // 3 for k in range(4)]
    parts = [(a * pk.unit, (b - a) * pk.unit) for a, b in zip(cuts, cuts[1:]) if b > a]
    weights = (
        jnp.pad(embed_weight, ((0, sh.cube), (0, 0))),
        norm_gain.reshape(1, width),
        attend_weight,
        output_weight,
        second_gain.reshape(1, width),
        expand_weight,
        reduce_weight,
        jnp.pad(decode_weight, ((0, 0), (0, sh.cube))),
    )
    ext_shape, inner_shape = (sh.ext, sh.feat), (sh.inner, sh.feat)
    slabs = sh.copies()
    sems = [pltpu.SemaphoreType.DMA((len(slabs),))] * 2
    slot_rows = sum(s[4] for s in slabs)

    def spread(u):
        return call(functools.partial(spread_kernel, sh, counts), [ext_shape], (u,), sems, 1)[0]

    def gather(back):
        scratch = [pltpu.VMEM((slot_rows, sh.feat), F32)] + sems
        return call(functools.partial(gather_kernel, sh, counts), [inner_shape], (back,), scratch, 2)[0]

    tokens_shape, query_shape = (sh.ext, width), (sh.inner, width)
    saved_shapes = [
        tokens_shape,
        query_shape,
        tokens_shape,
        tokens_shape,
        (HEADS * sh.inner, sh.ext),
        query_shape,
        query_shape,
        (sh.inner, hidden),
        query_shape,
    ]
    goal = to_tokens(sh, target)
    ext0 = spread(to_tokens(sh, field))
    new, *saved = call(functools.partial(first_kernel, sh), [inner_shape] + saved_shapes, (ext0,) + weights)
    ext1 = spread(new)
    packed_shape = (pk.rows, width)
    back, packed = call(functools.partial(middle_kernel, sh, pk), [ext_shape, packed_shape], (ext1, goal) + weights)
    cot = gather(back)
    back, packed = call(
        functools.partial(last_kernel, sh, pk),
        [ext_shape, packed_shape],
        (ext0, cot) + weights + tuple(saved) + (packed,),
    )
    cot = gather(back)
    steps = len(exchange_orders(counts)[0])
    summed = call(
        functools.partial(reduce_kernel, counts, parts),
        [packed_shape],
        (packed,),
        [
            pltpu.VMEM(packed_shape, F32),
            pltpu.VMEM(packed_shape, F32),
            pltpu.SemaphoreType.DMA((len(parts), 2 * steps)),
            pltpu.SemaphoreType.DMA((len(parts), 2 * steps)),
        ],
        3,
    )[0]
    entries = float(np.prod(field.shape) * devices)
    params = (embed_weight, norm_gain, attend_weight, output_weight, second_gain, expand_weight, reduce_weight, decode_weight)
    outs = [(1, 1), inner_shape] + [p.shape if p.ndim == 2 else (1, width) for p in params]
    done = call(functools.partial(finish_kernel, sh, pk, entries), outs, (summed, cot))
    grads = tuple(g.reshape(p.shape) for g, p in zip(done[2:], params))
    return (done[0].reshape(()), from_tokens(sh, done[1], field.shape)) + grads


def solution(mesh):
    counts = (mesh.shape["gx"], mesh.shape["gy"])
    in_specs = (P("gx", "gy", None), P("gx", "gy", None), P(), P(), P(), P(), P(), P(), P(), P())
    out_specs = (P(), P("gx", "gy", None), P(), P(), P(), P(), P(), P(), P(), P())
    return jax.shard_map(
        functools.partial(shards, counts), mesh=mesh, in_specs=in_specs, out_specs=out_specs, check_vma=False
    )
```

profile of v0, /device:TPU:0, one launch (start us, length us, event | category | flops | bytes accessed | tf_op | source)
XLA Modules:
  0.0 142.2 jit_solution(12056012700404048985)
XLA Ops:
  0.6 1.6 %pad.16.refs_1_.refs_2_ = f32[256,256]{1,0:T(8,128)} pad(f32[192,256]{1,0:T(8,128)} %param.12, f32[]{:T(128)} %constant.2.clone.1), padding=0_64x0_0 | pad | bytes 458756 | tf_op jit(solution)/shard_map/jit(_pad)/pad | solution.py:542
  2.3 1.1 copy.27
  3.4 0.0 copy-start
  3.4 0.7 pad.17.refs_8_.refs_9_
  4.1 1.7 %reshape.53 = f32[2,4,2,4,3,16,4]{6,5,4,3,2,1,0:T(8,128)S(1)} reshape(f32[8,8,192]{2,1,0:T(8,128)} %param.10) | data formatting | bytes 98304 | tf_op jit(solution)/shard_map/reshape | solution.py:524
  5.7 1.3 copy.25
  7.0 0.3 reshape.54
  7.4 0.1 copy.26
  7.5 0.6 pad.15.u
  8.1 11.2 %shard_map.177.refs_0_ = f32[256,256]{1,0:T(8,128)} custom-call(f32[64,256]{1,0:T(8,128)} %pad.15.u), custom_call_target="tpu_custom_call" | custom-call | tf_op jit(solution)/shard_map/pallas_call | solution.py:513
  19.4 0.0 copy-done
  19.4 0.8 reshape.57
  20.2 1.3 copy.28
  21.5 0.3 reshape.58
  21.8 0.1 copy.29
  21.9 0.6 pad.18.refs_1_
  22.5 5.6 %shard_map.178 = (f32[64,256]{1,0:T(8,128)}, f32[256,256]{1,0:T(8,128)}, f32[64,256]{1,0:T(8,128)}, f32[256,256]{1,0:T(8,128)}, f32[256,256]{1,0:T(8,128)}, /*in...) custom-call(f32[256,256]{1,0:T(8,128)} %shard_map.177.refs_0_, ...), custom_call_target="tpu_custom_call" | custom-call | tf_op jit(solution)/shard_map/pallas_call | solution.py:513
  28.2 9.6 %shard_map.179.refs_0_ = f32[256,256]{1,0:T(8,128)} custom-call(f32[64,256]{1,0:T(8,128)} %get-tuple-element.34.u), custom_call_target="tpu_custom_call" | custom-call | tf_op jit(solution)/shard_map/pallas_call | solution.py:513
  37.8 10.8 %shard_map.180 = (f32[256,256]{1,0:T(8,128)}, f32[2560,256]{1,0:T(8,128)}) custom-call(f32[256,256]{1,0:T(8,128)} %shard_map.179.refs_0_, f32[64,256]{1,0:T(8,128)} %pad.18.refs_1_, f32[256,256]{1,0:T(8,128)} %pad.16.refs_1_.refs_2_, f32[1,256]{1,0:T(1,128)} %bitcast.22, f32[256,768]{1,0:T(8,128)} %refs_4_.5, f32[256,256]{1,0:T(8,128)} %refs_5_.3, ...), custom_call_target="tpu_custom_call" | custom-call | tf_op jit(solution)/shard_map/pallas_call | solution.py:513
  48.6 9.7 %shard_map.181.refs_1_ = f32[64,256]{1,0:T(8,128)} custom-call(f32[256,256]{1,0:T(8,128)} %get-tuple-element.35.back), custom_call_target="tpu_custom_call" | custom-call | tf_op jit(solution)/shard_map/pallas_call | solution.py:513
  58.3 9.7 %shard_map.182 = (f32[256,256]{1,0:T(8,128)}, f32[2560,256]{1,0:T(8,128)}) custom-call(f32[256,256]{1,0:T(8,128)} %shard_map.177.refs_0_, f32[64,256]{1,0:T(8,128)} %shard_map.181.refs_1_, f32[256,256]{1,0:T(8,128)} %pad.16.refs_1_.refs_2_, f32[1,256]{1,0:T(1,128)} %bitcast.23, f32[256,768]{1,0:T(8,128)} %refs_4_.5, f32[256,256]{1,0:T(8,128)} %refs_5_.3, ...), custom_call_target="tpu_custom_call" | custom-call | tf_op jit(solution)/shard_map/pallas_call | solution.py:513
  68.0 55.3 %shard_map.183.packed = f32[2560,256]{1,0:T(8,128)} custom-call(f32[2560,256]{1,0:T(8,128)} %get-tuple-element.46.packed), custom_call_target="tpu_custom_call" | custom-call | tf_op jit(solution)/shard_map/pallas_call | solution.py:513
  123.3 10.0 %shard_map.184.cot = f32[64,256]{1,0:T(8,128)} custom-call(f32[256,256]{1,0:T(8,128)} %get-tuple-element.47.back), custom_call_target="tpu_custom_call" | custom-call | tf_op jit(solution)/shard_map/pallas_call | solution.py:513
  133.3 3.3 %shard_map.185 = (f32[1,1]{1,0:T(1,128)}, f32[64,256]{1,0:T(8,128)}, f32[192,256]{1,0:T(8,128)}, f32[1,256]{1,0:T(1,128)}, f32[256,768]{1,0:T(8,128)}, /*index=5...) custom-call(f32[2560,256]{1,0:T(8,128)} %shard_map.183.packed, ...), custom_call_target="tpu_custom_call" | custom-call | tf_op jit(solution)/shard_map/pallas_call | solution.py:513
  136.7 0.9 copy.30
  137.6 1.7 %copy.32 = f32[256,192]{0,1:T(8,128)} copy(f32[256,192]{1,0:T(8,128)} %get-tuple-element.77) | data formatting | bytes 393216
  139.4 0.3 reshape.60
  139.7 1.2 copy.31
  140.9 1.3 reshape.61
Async XLA Ops:
  3.4 16.0 %copy-start = (f32[8,8,192]{2,1,0:T(8,128)S(1)}, f32[8,8,192]{2,1,0:T(8,128)}, u32[]{:S(2)}) copy-start(f32[8,8,192]{2,1,0:T(8,128)} %param.11) | copy-start | bytes 147460
where the time goes:
time: 143 us; the launch traced here: 142 us
  Pallas kernels  125 us (87%)
  local copies, waits for them, and re-layouts  16.1 us (11%)
    pallas_call x9, Pallas kernels, call(): pl.pallas_call(kernel, out_shape=[jax.ShapeDtypeStruct(s, F32) for s in o...  125 us

commit v1 on v0

--- a/solution.py
+++ b/solution.py
@@ -388,6 +388,27 @@
 
 def gather_kernel(sh, counts, back, out, slots, send, recv):
     greet([neighbour(counts, dx, dy) for dx, dy in AROUND])
+    end_gather(sh, back, out, slots, start_gather(sh, counts, back, slots, send, recv))
+
+
+def exchange_orders(counts):
+    nx, ny = counts
+    bits = lambda n: [1 << k for k in range(n.bit_length() - 1)]
+    ys = [("gy", s) for s in bits(ny)]
+    xs = [("gx", s) for s in bits(nx)]
+    head, y, x, z = ys[:1], ys[1:], xs[:1], xs[1:]
+    return [head + y + x + z, head + x + z + y, head + z + y + x]
+
+
+def partner(axis, s):
+    gx, gy = lax.axis_index("gx"), lax.axis_index("gy")
+    index = gx if axis == "gx" else gy
+    bit = lax.rem(index // s, 2)
+    other = index + s - 2 * s * bit
+    return bit, ((other, gy) if axis == "gx" else (gx, other))
+
+
+def start_gather(sh, counts, back, slots, send, recv):
     started = []
     place = 0
     for i, (dx, dy, dst, src, n) in enumerate(sh.copies()):
@@ -402,6 +423,10 @@
         copy.start()
         started.append((copy, dst, place, n))
         place += n
+    return started
+
+
+def end_gather(sh, back, out, slots, started):
     at = 0
     for s, n in sh.view(0, 0):
         out[at : at + n, :] = back[s : s + n, :]
@@ -411,74 +436,69 @@
         out[dst : dst + n, :] += slots[place : place + n, :]
 
 
-def exchange_orders(counts):
-    nx, ny = counts
-    bits = lambda n: [1 << k for k in range(n.bit_length() - 1)]
-    ys = [("gy", s) for s in bits(ny)]
-    xs = [("gx", s) for s in bits(nx)]
-    head, y, x, z = ys[:1], ys[1:], xs[:1], xs[1:]
-    return [head + y + x + z, head + x + z + y, head + z + y + x]
-
-
-def partner(axis, s):
-    gx, gy = lax.axis_index("gx"), lax.axis_index("gy")
-    index = gx if axis == "gx" else gy
-    bit = lax.rem(index // s, 2)
-    other = index + s - 2 * s * bit
-    return bit, ((other, gy) if axis == "gx" else (gx, other))
-
-
-def reduce_kernel(counts, parts, packed, out, acc, slots, send, recv):
+def reduce_kernel(sh, counts, parts, packed, back, out, cot, acc, slots, halo, send, recv, halo_send, halo_recv):
     orders = exchange_orders(counts)
-    greet([partner(*step)[1] for step in orders[0]])
+    greet([neighbour(counts, dx, dy) for dx, dy in AROUND] + [partner(*step)[1] for step in orders[0]])
+    halos = start_gather(sh, counts, back, halo, halo_send, halo_recv)
     steps = len(orders[0])
     where = []
     base = 0
-    for start, rows in parts:
-        where.append([start, rows, base])
+    for order, start, rows in parts:
+        where.append((start, rows, base))
         base += rows
-    source = packed
     history = [[] for _ in parts]
+
+    def halve(p, k):
+        start, rows, base = where[p]
+        bit, device = partner(*orders[parts[p][0]][k])
+        half = rows // 2
+        keep = pl.multiple_of(start + bit * half, 8)
+        give = pl.multiple_of(start + half - bit * half, 8)
+        source = packed if k == 0 else acc
+        copy = pltpu.make_async_remote_copy(
+            src_ref=source.at[pl.ds(give, half)],
+            dst_ref=slots.at[pl.ds(base, half)],
+            send_sem=send.at[p, k],
+            recv_sem=recv.at[p, k],
+            device_id=device,
+            device_id_type=MESH,
+        )
+        copy.start()
+        history[p].append((keep, half, device))
+        return copy, source, keep, half, base
+
+    def add(p, k, flight):
+        copy, source, keep, half, base = flight
+        copy.wait()
+        target = acc if k < steps - 1 else out
+        target[pl.ds(keep, half), :] = source[pl.ds(keep, half), :] + slots[pl.ds(base, half), :]
+        where[p] = (keep, half, base + half)
+
+    def collect(p, k):
+        keep, half, device = history[p][k]
+        copy = pltpu.make_async_remote_copy(
+            src_ref=out.at[pl.ds(keep, half)],
+            dst_ref=out.at[pl.ds(keep, half)],
+            send_sem=send.at[p, steps + k],
+            recv_sem=recv.at[p, steps + k],
+            device_id=device,
+            device_id_type=MESH,
+        )
+        copy.start()
+        return copy
+
+    every = range(len(parts))
+    flights = [halve(p, 0) for p in every]
+    end_gather(sh, back, cot, halo, halos)
     for k in range(steps):
-        flight = []
-        for p, (start, rows, base) in enumerate(where):
-            bit, device = partner(*orders[p][k])
-            half = rows // 2
-            keep = pl.multiple_of(start + bit * half, 8)
-            give = pl.multiple_of(start + half - bit * half, 8)
-            copy = pltpu.make_async_remote_copy(
-                src_ref=source.at[pl.ds(give, half)],
-                dst_ref=slots.at[pl.ds(base, half)],
-                send_sem=send.at[p, k],
-                recv_sem=recv.at[p, k],
-                device_id=device,
-                device_id_type=MESH,
-            )
-            copy.start()
-            flight.append((copy, keep, half, base))
-            history[p].append((keep, half, device))
-        for p, (copy, keep, half, base) in enumerate(flight):
-            copy.wait()
-            target = acc if k < steps - 1 else out
-            target[pl.ds(keep, half), :] = source[pl.ds(keep, half), :] + slots[pl.ds(base, half), :]
-            where[p] = [keep, half, base + half]
-        source = acc
+        for p in every:
+            add(p, k, flights[p])
+            flights[p] = halve(p, k + 1) if k < steps - 1 else collect(p, k)
     for k in reversed(range(steps)):
-        flight = []
-        for p in range(len(parts)):
-            keep, half, device = history[p][k]
-            copy = pltpu.make_async_remote_copy(
-                src_ref=out.at[pl.ds(keep, half)],
-                dst_ref=out.at[pl.ds(keep, half)],
-                send_sem=send.at[p, steps + k],
-                recv_sem=recv.at[p, steps + k],
-                device_id=device,
-                device_id_type=MESH,
-            )
-            copy.start()
-            flight.append(copy)
-        for copy in flight:
-            copy.wait()
+        for p in every:
+            flights[p].wait()
+            if k > 0:
+                flights[p] = collect(p, k - 1)
 
 
 def finish_kernel(sh, pk, entries, packed, cot, loss, field, embed, norm, attend, output, second, expand, reduce, decode):
@@ -536,8 +556,9 @@
     devices = counts[0] * counts[1]
     pk = Packing(sh, devices)
     blocks = pk.rows // pk.unit
-    cuts = [blocks * k // 3 for k in range(4)]
-    parts = [(a * pk.unit, (b - a) * pk.unit) for a, b in zip(cuts, cuts[1:]) if b > a]
+    cuts = [blocks * share // 10 for share in (0, 3, 5, 7, 8, 9, 10)]
+    spans = zip((0, 1, 0, 2, 1, 2), cuts, cuts[1:])
+    parts = [(order, a * pk.unit, (b - a) * pk.unit) for order, a, b in spans if b > a]
     weights = (
         jnp.pad(embed_weight, ((0, sh.cube), (0, 0))),
         norm_gain.reshape(1, width),
@@ -584,20 +605,20 @@
         [ext_shape, packed_shape],
         (ext0, cot) + weights + tuple(saved) + (packed,),
     )
-    cot = gather(back)
     steps = len(exchange_orders(counts)[0])
-    summed = call(
-        functools.partial(reduce_kernel, counts, parts),
-        [packed_shape],
-        (packed,),
+    summed, cot = call(
+        functools.partial(reduce_kernel, sh, counts, parts),
+        [packed_shape, inner_shape],
+        (packed, back),
         [
             pltpu.VMEM(packed_shape, F32),
             pltpu.VMEM(packed_shape, F32),
-            pltpu.SemaphoreType.DMA((len(parts), 2 * steps)),
-            pltpu.SemaphoreType.DMA((len(parts), 2 * steps)),
-        ],
+            pltpu.VMEM((slot_rows, sh.feat), F32),
+        ]
+        + [pltpu.SemaphoreType.DMA((len(parts), 2 * steps))] * 2
+        + sems,
         3,
-    )[0]
+    )
     entries = float(np.prod(field.shape) * devices)
     params = (embed_weight, norm_gain, attend_weight, output_weight, second_gain, expand_weight, reduce_weight, decode_weight)
     outs = [(1, 1), inner_shape] + [p.shape if p.ndim == 2 else (1, width) for p in params]

time: 143 us -> 128 us (0.90)
  Pallas kernels: 125 us -> 110 us
    pallas_call x9 -> x8, Pallas kernels: 125 us -> 110 us  [call(): pl.pallas_call(kernel, out_shape=[jax.ShapeDtypeStruct(s, F32) for s in o...]
where the time goes in v1:
time: 128 us; the launch traced here: 127 us
  Pallas kernels  110 us (86%)
  local copies, waits for them, and re-layouts  16.1 us (13%)
    pallas_call x8, Pallas kernels, call(): pl.pallas_call(kernel, out_shape=[jax.ShapeDtypeStruct(s, F32) for s in o...  110 us
    unnamed x4, local copies, waits for them, and re-layouts  2.81 us
    transpose x2, local copies, waits for them, and re-layouts, to_tokens(): block.reshape(sh.ax, PATCH, sh.ay, PATCH, 3, sh.up, PATCH)  2.59 us

profile of v1, /device:TPU:0, one launch (start us, length us, event | category | flops | bytes accessed | tf_op | source)
XLA Modules:
  0.0 127.0 jit_solution(4719659409999705817)
XLA Ops:
  0.6 1.6 %pad.16.refs_1_.refs_2_ = f32[256,256]{1,0:T(8,128)} pad(f32[192,256]{1,0:T(8,128)} %param.12, f32[]{:T(128)} %constant.2.clone.1), padding=0_64x0_0 | pad | bytes 458756 | tf_op jit(solution)/shard_map/jit(_pad)/pad | solution.py:563
  2.3 1.1 copy.27
  3.4 0.0 copy-start
  3.4 0.7 pad.17.refs_8_.refs_9_
  4.1 1.7 %reshape.53 = f32[2,4,2,4,3,16,4]{6,5,4,3,2,1,0:T(8,128)S(1)} reshape(f32[8,8,192]{2,1,0:T(8,128)} %param.10) | data formatting | bytes 98304 | tf_op jit(solution)/shard_map/reshape | solution.py:544
  5.7 1.3 %copy.25 = f32[2,2,16,3,4,4,4]{2,1,0,6,5,4,3:T(2,128)S(1)} copy(f32[2,2,16,3,4,4,4]{6,2,3,5,1,4,0:T(8,128)S(1)} %bitcast.17) | data formatting | bytes 98304 | tf_op jit(solution)/shard_map/transpose | solution.py:544
  7.0 0.3 reshape.54
  7.4 0.1 copy.26
  7.5 0.6 pad.15.u
  8.1 11.2 %shard_map.177.refs_0_ = f32[256,256]{1,0:T(8,128)} custom-call(f32[64,256]{1,0:T(8,128)} %pad.15.u), custom_call_target="tpu_custom_call" | custom-call | tf_op jit(solution)/shard_map/pallas_call | solution.py:533
  19.4 0.0 copy-done
  19.4 0.8 reshape.57
  20.2 1.3 %copy.28 = f32[2,2,16,3,4,4,4]{2,1,0,6,5,4,3:T(2,128)S(1)} copy(f32[2,2,16,3,4,4,4]{6,2,3,5,1,4,0:T(8,128)S(1)} %bitcast.18) | data formatting | bytes 98304 | tf_op jit(solution)/shard_map/transpose | solution.py:544
  21.5 0.3 reshape.58
  21.8 0.1 copy.29
  21.9 0.6 pad.18.refs_1_
  22.5 5.6 %shard_map.178 = (f32[64,256]{1,0:T(8,128)}, f32[256,256]{1,0:T(8,128)}, f32[64,256]{1,0:T(8,128)}, f32[256,256]{1,0:T(8,128)}, f32[256,256]{1,0:T(8,128)}, /*in...) custom-call(f32[256,256]{1,0:T(8,128)} %shard_map.177.refs_0_, ...), custom_call_target="tpu_custom_call" | custom-call | tf_op jit(solution)/shard_map/pallas_call | solution.py:533
  28.2 9.6 %shard_map.179.refs_0_ = f32[256,256]{1,0:T(8,128)} custom-call(f32[64,256]{1,0:T(8,128)} %get-tuple-element.36.u), custom_call_target="tpu_custom_call" | custom-call | tf_op jit(solution)/shard_map/pallas_call | solution.py:533
  37.8 10.8 %shard_map.180 = (f32[256,256]{1,0:T(8,128)}, f32[2560,256]{1,0:T(8,128)}) custom-call(f32[256,256]{1,0:T(8,128)} %shard_map.179.refs_0_, f32[64,256]{1,0:T(8,128)} %pad.18.refs_1_, f32[256,256]{1,0:T(8,128)} %pad.16.refs_1_.refs_2_, f32[1,256]{1,0:T(1,128)} %bitcast.22, f32[256,768]{1,0:T(8,128)} %refs_4_.5, f32[256,256]{1,0:T(8,128)} %refs_5_.3, ...), custom_call_target="tpu_custom_call" | custom-call | tf_op jit(solution)/shard_map/pallas_call | solution.py:533
  48.6 9.7 %shard_map.181.refs_1_ = f32[64,256]{1,0:T(8,128)} custom-call(f32[256,256]{1,0:T(8,128)} %get-tuple-element.37.back), custom_call_target="tpu_custom_call" | custom-call | tf_op jit(solution)/shard_map/pallas_call | solution.py:533
  58.3 9.7 %shard_map.182 = (f32[256,256]{1,0:T(8,128)}, f32[2560,256]{1,0:T(8,128)}) custom-call(f32[256,256]{1,0:T(8,128)} %shard_map.177.refs_0_, f32[64,256]{1,0:T(8,128)} %shard_map.181.refs_1_, f32[256,256]{1,0:T(8,128)} %pad.16.refs_1_.refs_2_, f32[1,256]{1,0:T(1,128)} %bitcast.23, f32[256,768]{1,0:T(8,128)} %refs_4_.5, f32[256,256]{1,0:T(8,128)} %refs_5_.3, ...), custom_call_target="tpu_custom_call" | custom-call | tf_op jit(solution)/shard_map/pallas_call | solution.py:533
  68.0 50.1 %shard_map.183 = (f32[2560,256]{1,0:T(8,128)}, f32[64,256]{1,0:T(8,128)}) custom-call(f32[2560,256]{1,0:T(8,128)} %get-tuple-element.48.packed, f32[256,256]{1,0:T(8,128)} %get-tuple-element.49.back), custom_call_target="tpu_custom_call" | custom-call | tf_op jit(solution)/shard_map/pallas_call | solution.py:533
  118.2 3.3 %shard_map.184 = (f32[1,1]{1,0:T(1,128)}, f32[64,256]{1,0:T(8,128)}, f32[192,256]{1,0:T(8,128)}, f32[1,256]{1,0:T(1,128)}, f32[256,768]{1,0:T(8,128)}, /*index=5...) custom-call(f32[2560,256]{1,0:T(8,128)} %get-tuple-element.50.packed, ...), custom_call_target="tpu_custom_call" | custom-call | tf_op jit(solution)/shard_map/pallas_call | solution.py:533
  121.5 0.9 copy.30
  122.4 1.7 %copy.32 = f32[256,192]{0,1:T(8,128)} copy(f32[256,192]{1,0:T(8,128)} %get-tuple-element.81) | data formatting | bytes 393216
  124.2 0.3 reshape.60
  124.5 1.2 copy.31
  125.7 1.3 reshape.61
Async XLA Ops:
  3.4 16.0 %copy-start = (f32[8,8,192]{2,1,0:T(8,128)S(1)}, f32[8,8,192]{2,1,0:T(8,128)}, u32[]{:S(2)}) copy-start(f32[8,8,192]{2,1,0:T(8,128)} %param.11) | copy-start | bytes 147460

commit v2 on v1

--- a/solution.py
+++ b/solution.py
@@ -316,36 +316,6 @@
     return emit
 
 
-def first_kernel(sh, *refs):
-    ext, w, (new, *saved) = refs[0], refs[1:9], refs[9:]
-    e = ext[...]
-    closed, kept = forward(sh, e, w)
-    new[...] = stencil(sh, e, closed)
-    for ref, value in zip(saved, kept):
-        ref[...] = value
-
-
-def middle_kernel(sh, pk, *refs):
-    ext, target, w, (back, packed) = refs[0], refs[1], refs[2:10], refs[10:12]
-    packed[pk.at["small"][0] :, :] = jnp.zeros((pk.rows - pk.at["small"][0], sh.width), F32)
-    emit = make_emit(sh, pk, packed, None)
-    e = ext[...]
-    closed, kept = forward(sh, e, w)
-    goal = target[...]
-    residue = stencil(sh, e, closed) - goal
-    emit("misfit", jnp.sum(residue * residue, axis=0, keepdims=True))
-    emit("energy", jnp.sum(goal * goal, axis=0, keepdims=True))
-    backward(sh, e, w, kept, 2.0 * residue, back, emit)
-
-
-def last_kernel(sh, pk, *refs):
-    ext, cot, w, saved, prior, (back, packed) = refs[0], refs[1], refs[2:10], refs[10:19], refs[19], refs[20:22]
-    packed[pk.at["small"][0] :, :] = prior[pk.at["small"][0] :, :]
-    emit = make_emit(sh, pk, packed, prior)
-    kept = tuple(ref[...] for ref in saved)
-    backward(sh, ext[...], w, kept, cot[...], back, emit)
-
-
 def neighbour(counts, dx, dy):
     nx, ny = counts
     return (
@@ -364,8 +334,7 @@
 AROUND = [(dx, dy) for dx in (-1, 0, 1) for dy in (-1, 0, 1) if (dx, dy) != (0, 0)]
 
 
-def spread_kernel(sh, counts, u, ext, send, recv):
-    greet([neighbour(counts, dx, dy) for dx, dy in AROUND])
+def spread(sh, counts, u, ext, send, recv):
     started = []
     for i, (dx, dy, src, dst, n) in enumerate(sh.copies()):
         copy = pltpu.make_async_remote_copy(
@@ -386,11 +355,6 @@
         copy.wait()
 
 
-def gather_kernel(sh, counts, back, out, slots, send, recv):
-    greet([neighbour(counts, dx, dy) for dx, dy in AROUND])
-    end_gather(sh, back, out, slots, start_gather(sh, counts, back, slots, send, recv))
-
-
 def exchange_orders(counts):
     nx, ny = counts
     bits = lambda n: [1 << k for k in range(n.bit_length() - 1)]
@@ -436,10 +400,26 @@
         out[dst : dst + n, :] += slots[place : place + n, :]
 
 
-def reduce_kernel(sh, counts, parts, packed, back, out, cot, acc, slots, halo, send, recv, halo_send, halo_recv):
+def steps_kernel(sh, pk, counts, parts, *refs):
+    u0, goal, w, (out, cot0) = refs[0], refs[1], refs[2:10], refs[10:12]
+    ext0, ext1, u1, back1, back0, cot1, packed, acc, slots, halo1, halo0 = refs[12:23]
+    saved, (send, recv, spread_send, spread_recv, gather_send, gather_recv) = refs[23:32], refs[32:38]
     orders = exchange_orders(counts)
     greet([neighbour(counts, dx, dy) for dx, dy in AROUND] + [partner(*step)[1] for step in orders[0]])
-    halos = start_gather(sh, counts, back, halo, halo_send, halo_recv)
+    spread(sh, counts, u0, ext0, spread_send.at[0], spread_recv.at[0])
+    closed, kept = forward(sh, ext0[...], w)
+    u1[...] = stencil(sh, ext0[...], closed)
+    for ref, value in zip(saved, kept):
+        ref[...] = value
+    spread(sh, counts, u1, ext1, spread_send.at[1], spread_recv.at[1])
+    packed[pk.at["small"][0] :, :] = jnp.zeros((pk.rows - pk.at["small"][0], sh.width), F32)
+    emit = make_emit(sh, pk, packed, None)
+    closed, kept = forward(sh, ext1[...], w)
+    residue = stencil(sh, ext1[...], closed) - goal[...]
+    emit("misfit", jnp.sum(residue * residue, axis=0, keepdims=True))
+    emit("energy", jnp.sum(goal[...] * goal[...], axis=0, keepdims=True))
+    backward(sh, ext1[...], w, kept, 2.0 * residue, back1, emit)
+    end_gather(sh, back1, cot1, halo1, start_gather(sh, counts, back1, halo1, gather_send.at[0], gather_recv.at[0]))
     steps = len(orders[0])
     where = []
     base = 0
@@ -488,10 +468,31 @@
         return copy
 
     every = range(len(parts))
-    flights = [halve(p, 0) for p in every]
-    end_gather(sh, back, cot, halo, halos)
+    first = pk.at["query"][0]
+    early = [p for p in every if parts[p][1] + parts[p][2] <= first]
+    flights = {}
+    emit = make_emit(sh, pk, packed, packed)
+
+    def emit_and_send(name, value):
+        emit(name, value)
+        if name == "output":
+            for p in early:
+                flights[p] = halve(p, 0)
+        if name == "query":
+            for p in early:
+                add(p, 0, flights[p])
+                flights[p] = halve(p, 1)
+
+    backward(sh, ext0[...], w, tuple(ref[...] for ref in saved), cot1[...], back0, emit_and_send)
+    halos = start_gather(sh, counts, back0, halo0, gather_send.at[1], gather_recv.at[1])
+    for p in every:
+        if p not in early:
+            flights[p] = halve(p, 0)
+    end_gather(sh, back0, cot0, halo0, halos)
     for k in range(steps):
         for p in every:
+            if k == 0 and p in early:
+                continue
             add(p, k, flights[p])
             flights[p] = halve(p, k + 1) if k < steps - 1 else collect(p, k)
     for k in reversed(range(steps)):
@@ -556,8 +557,8 @@
     devices = counts[0] * counts[1]
     pk = Packing(sh, devices)
     blocks = pk.rows // pk.unit
-    cuts = [blocks * share // 10 for share in (0, 3, 5, 7, 8, 9, 10)]
-    spans = zip((0, 1, 0, 2, 1, 2), cuts, cuts[1:])
+    cuts = [blocks * share // 10 for share in (0, 3, 5, 6, 8, 9, 10)]
+    spans = zip((0, 1, 2, 0, 1, 2), cuts, cuts[1:])
     parts = [(order, a * pk.unit, (b - a) * pk.unit) for order, a, b in spans if b > a]
     weights = (
         jnp.pad(embed_weight, ((0, sh.cube), (0, 0))),
@@ -571,16 +572,8 @@
     )
     ext_shape, inner_shape = (sh.ext, sh.feat), (sh.inner, sh.feat)
     slabs = sh.copies()
-    sems = [pltpu.SemaphoreType.DMA((len(slabs),))] * 2
-    slot_rows = sum(s[4] for s in slabs)
-
-    def spread(u):
-        return call(functools.partial(spread_kernel, sh, counts), [ext_shape], (u,), sems, 1)[0]
-
-    def gather(back):
-        scratch = [pltpu.VMEM((slot_rows, sh.feat), F32)] + sems
-        return call(functools.partial(gather_kernel, sh, counts), [inner_shape], (back,), scratch, 2)[0]
-
+    sems = [pltpu.SemaphoreType.DMA((2, len(slabs)))] * 4
+    slot_rows = sum(n[4] for n in slabs)
     tokens_shape, query_shape = (sh.ext, width), (sh.inner, width)
     saved_shapes = [
         tokens_shape,
@@ -594,30 +587,19 @@
         query_shape,
     ]
     goal = to_tokens(sh, target)
-    ext0 = spread(to_tokens(sh, field))
-    new, *saved = call(functools.partial(first_kernel, sh), [inner_shape] + saved_shapes, (ext0,) + weights)
-    ext1 = spread(new)
     packed_shape = (pk.rows, width)
-    back, packed = call(functools.partial(middle_kernel, sh, pk), [ext_shape, packed_shape], (ext1, goal) + weights)
-    cot = gather(back)
-    back, packed = call(
-        functools.partial(last_kernel, sh, pk),
-        [ext_shape, packed_shape],
-        (ext0, cot) + weights + tuple(saved) + (packed,),
-    )
     steps = len(exchange_orders(counts)[0])
+    halo_shape = (slot_rows, sh.feat)
+    scratch = [ext_shape, ext_shape, inner_shape, ext_shape, ext_shape, inner_shape] + [packed_shape] * 3
+    scratch += [halo_shape] * 2 + saved_shapes
     summed, cot = call(
-        functools.partial(reduce_kernel, sh, counts, parts),
+        functools.partial(steps_kernel, sh, pk, counts, parts),
         [packed_shape, inner_shape],
-        (packed, back),
-        [
-            pltpu.VMEM(packed_shape, F32),
-            pltpu.VMEM(packed_shape, F32),
-            pltpu.VMEM((slot_rows, sh.feat), F32),
-        ]
+        (to_tokens(sh, field), goal) + weights,
+        [pltpu.VMEM(shape, F32) for shape in scratch]
         + [pltpu.SemaphoreType.DMA((len(parts), 2 * steps))] * 2
         + sems,
-        3,
+        1,
     )
     entries = float(np.prod(field.shape) * devices)
     params = (embed_weight, norm_gain, attend_weight, output_weight, second_gain, expand_weight, reduce_weight, decode_weight)

time: 128 us -> 101 us (0.79)
  Pallas kernels: 110 us -> 84.2 us
    pallas_call x8 -> x2, Pallas kernels: 110 us -> 84.2 us  [call(): pl.pallas_call(kernel, out_shape=[jax.ShapeDtypeStruct(s, F32) for s in o...]
where the time goes in v2:
time: 101 us
  Pallas kernels  84.2 us (83%)
  local copies, waits for them, and re-layouts  16.1 us (16%)
    pallas_call x2, Pallas kernels, call(): pl.pallas_call(kernel, out_shape=[jax.ShapeDtypeStruct(s, F32) for s in o...  84.2 us
    unnamed x4, local copies, waits for them, and re-layouts  2.81 us
    transpose x2, local copies, waits for them, and re-layouts, to_tokens(): block.reshape(sh.ax, PATCH, sh.ay, PATCH, 3, sh.up, PATCH)  2.58 us
    reshape x2, local copies, waits for them, and re-layouts, to_tokens(): block.reshape(sh.ax, PATCH, sh.ay, PATCH, 3, sh.up, PATCH)  2.46 us

profile of v2, /device:TPU:0, one launch (start us, length us, event | category | flops | bytes accessed | tf_op | source)
XLA Modules:
  0.0 101.0 jit_solution(6449267303627380563)
XLA Ops:
  0.6 1.6 %pad.17.refs_2_ = f32[256,256]{1,0:T(8,128)} pad(f32[192,256]{1,0:T(8,128)} %param.12, f32[]{:T(128)} %constant.2.clone.1), padding=0_64x0_0 | pad | bytes 458756 | tf_op jit(solution)/shard_map/jit(_pad)/pad | solution.py:564
  2.3 1.1 %copy.29 = f32[256,192]{1,0:T(8,128)S(1)} copy(f32[256,192]{0,1:T(8,128)} %param.19) | data formatting | bytes 393216 | tf_op args[9]
  3.4 0.7 pad.18.refs_9_
  4.1 1.7 %reshape.53 = f32[2,4,2,4,3,16,4]{6,5,4,3,2,1,0:T(8,128)S(1)} reshape(f32[8,8,192]{2,1,0:T(8,128)} %param.10) | data formatting | bytes 98304 | tf_op jit(solution)/shard_map/reshape | solution.py:545
  5.7 0.0 copy-start
  5.7 1.3 %copy.25 = f32[2,2,16,3,4,4,4]{2,1,0,6,5,4,3:T(2,128)S(1)} copy(f32[2,2,16,3,4,4,4]{6,2,3,5,1,4,0:T(8,128)S(1)} %bitcast.17) | data formatting | bytes 98304 | tf_op jit(solution)/shard_map/transpose | solution.py:545
  7.0 0.3 reshape.54
  7.4 0.1 copy.26
  7.5 0.6 pad.15.refs_0_
  8.1 0.0 copy-done
  8.1 0.8 reshape.55
  8.9 1.3 %copy.27 = f32[2,2,16,3,4,4,4]{2,1,0,6,5,4,3:T(2,128)S(1)} copy(f32[2,2,16,3,4,4,4]{6,2,3,5,1,4,0:T(8,128)S(1)} %bitcast.18) | data formatting | bytes 98304 | tf_op jit(solution)/shard_map/transpose | solution.py:545
  10.2 0.3 reshape.56
  10.6 0.1 copy.28
  10.6 0.6 pad.16.refs_1_
  11.3 80.8 %shard_map.177 = (f32[2560,256]{1,0:T(8,128)}, f32[64,256]{1,0:T(8,128)}) custom-call(f32[64,256]{1,0:T(8,128)} %pad.15.refs_0_, f32[64,256]{1,0:T(8,128)} %pad.16.refs_1_, f32[256,256]{1,0:T(8,128)} %pad.17.refs_2_, f32[1,256]{1,0:T(1,128)} %bitcast.21, f32[256,768]{1,0:T(8,128)} %refs_4_.1, f32[256,256]{1,0:T(8,128)} %refs_5_.1, f32[1,256]{1,0:T(1,128)} %bitcast.22, ...), custom_call_target="tpu_custom_call" | custom-call | tf_op jit(solution)/shard_map/pallas_call | solution.py:534
  92.1 3.3 %shard_map.178 = (f32[1,1]{1,0:T(1,128)}, f32[64,256]{1,0:T(8,128)}, f32[192,256]{1,0:T(8,128)}, f32[1,256]{1,0:T(1,128)}, f32[256,768]{1,0:T(8,128)}, /*index=5...) custom-call(f32[2560,256]{1,0:T(8,128)} %get-tuple-element.22.packed, ...), custom_call_target="tpu_custom_call" | custom-call | tf_op jit(solution)/shard_map/pallas_call | solution.py:534
  95.5 0.9 copy.30
  96.4 1.7 %copy.32 = f32[256,192]{0,1:T(8,128)} copy(f32[256,192]{1,0:T(8,128)} %get-tuple-element.53) | data formatting | bytes 393216
  98.1 0.3 reshape.60
  98.5 1.2 %copy.31 = f32[2,4,2,4,3,16,4]{6,5,4,3,2,1,0:T(8,128)S(1)} copy(f32[2,4,2,4,3,16,4]{5,2,0,6,3,1,4:T(2,128)S(1)} %bitcast.19) | data formatting | bytes 98304 | tf_op jit(solution)/shard_map/transpose | solution.py:551
  99.7 1.3 %reshape.61 = f32[8,8,192]{2,1,0:T(8,128)} reshape(f32[2,4,2,4,3,16,4]{6,5,4,3,2,1,0:T(8,128)S(1)} %copy.31) | data formatting | bytes 98304 | tf_op jit(solution)/shard_map/reshape | solution.py:551
Async XLA Ops:
  5.7 2.4 %copy-start = (f32[8,8,192]{2,1,0:T(8,128)S(1)}, f32[8,8,192]{2,1,0:T(8,128)}, u32[]{:S(2)}) copy-start(f32[8,8,192]{2,1,0:T(8,128)} %param.11) | copy-start | bytes 147460

commit v3 on v2

--- a/solution.py
+++ b/solution.py
@@ -403,7 +403,13 @@
 def steps_kernel(sh, pk, counts, parts, *refs):
     u0, goal, w, (out, cot0) = refs[0], refs[1], refs[2:10], refs[10:12]
     ext0, ext1, u1, back1, back0, cot1, packed, acc, slots, halo1, halo0 = refs[12:23]
-    saved, (send, recv, spread_send, spread_recv, gather_send, gather_recv) = refs[23:32], refs[32:38]
+    saved, wide, sems = refs[23:32], refs[32:36], refs[36:42]
+    send, recv, spread_send, spread_recv, gather_send, gather_recv = sems
+    for ref, value in zip(wide, (u0, goal, w[0], w[7])):
+        ref[...] = jnp.zeros(ref.shape, F32)
+        ref[: value.shape[0], : value.shape[1]] = value[...]
+    u0, goal = wide[:2]
+    w = (wide[2],) + tuple(w[1:7]) + (wide[3],)
     orders = exchange_orders(counts)
     greet([neighbour(counts, dx, dy) for dx, dy in AROUND] + [partner(*step)[1] for step in orders[0]])
     spread(sh, counts, u0, ext0, spread_send.at[0], spread_recv.at[0])
@@ -543,7 +549,7 @@
 
 def to_tokens(sh, block):
     x = block.reshape(sh.ax, PATCH, sh.ay, PATCH, 3, sh.up, PATCH).transpose(0, 2, 5, 4, 1, 3, 6)
-    return jnp.pad(x.reshape(sh.inner, 3 * sh.cube), ((0, 0), (0, sh.cube)))
+    return x.reshape(sh.inner, 3 * sh.cube)
 
 
 def from_tokens(sh, tokens, shape):
@@ -561,14 +567,14 @@
     spans = zip((0, 1, 2, 0, 1, 2), cuts, cuts[1:])
     parts = [(order, a * pk.unit, (b - a) * pk.unit) for order, a, b in spans if b > a]
     weights = (
-        jnp.pad(embed_weight, ((0, sh.cube), (0, 0))),
+        embed_weight,
         norm_gain.reshape(1, width),
         attend_weight,
         output_weight,
         second_gain.reshape(1, width),
         expand_weight,
         reduce_weight,
-        jnp.pad(decode_weight, ((0, 0), (0, sh.cube))),
+        decode_weight,
     )
     ext_shape, inner_shape = (sh.ext, sh.feat), (sh.inner, sh.feat)
     slabs = sh.copies()
@@ -592,6 +598,7 @@
     halo_shape = (slot_rows, sh.feat)
     scratch = [ext_shape, ext_shape, inner_shape, ext_shape, ext_shape, inner_shape] + [packed_shape] * 3
     scratch += [halo_shape] * 2 + saved_shapes
+    scratch += [inner_shape, inner_shape, (sh.feat, width), (width, sh.feat)]
     summed, cot = call(
         functools.partial(steps_kernel, sh, pk, counts, parts),
         [packed_shape, inner_shape],

time: 101 us -> 99.2 us (0.982)
  local copies, waits for them, and re-layouts: 16.1 us -> 14.4 us
    pad x4 -> x0, local copies, waits for them, and re-layouts: 3.64 us -> none  [the longest x1 1.65 us: shards(): jnp.pad(embed_weight, ((0, sh.cube), (0, 0)))]
    reshape x4, local copies, waits for them, and re-layouts: 0.85 us -> 2.11 us  [to_tokens(): return x.reshape(sh.inner, 3 * sh.cube)]
where the time goes in v3:
time: 99.2 us; the launch traced here: 98.7 us
  Pallas kernels  83.6 us (84%)
  local copies, waits for them, and re-layouts  14.4 us (15%)
    pallas_call x2, Pallas kernels, call(): pl.pallas_call(kernel, out_shape=[jax.ShapeDtypeStruct(s, F32) for s in o...  83.6 us
    unnamed x4, local copies, waits for them, and re-layouts  3.52 us
    transpose x2, local copies, waits for them, and re-layouts, to_tokens(): block.reshape(sh.ax, PATCH, sh.ay, PATCH, 3, sh.up, PATCH)  2.58 us
    reshape x2, local copies, waits for them, and re-layouts, to_tokens(): block.reshape(sh.ax, PATCH, sh.ay, PATCH, 3, sh.up, PATCH)  2.46 us
    reshape x4, local copies, waits for them, and re-layouts, to_tokens(): return x.reshape(sh.inner, 3 * sh.cube)  2.11 us

profile of v3, /device:TPU:0, one launch (start us, length us, event | category | flops | bytes accessed | tf_op | source)
XLA Modules:
  0.0 98.7 jit_solution(11641953415324692440)
XLA Ops:
  0.6 1.8 %copy.29.refs_9_ = f32[256,192]{1,0:T(8,128)} copy(f32[256,192]{0,1:T(8,128)} %param.19) | data formatting | bytes 393216 | tf_op args[9]
  2.4 1.7 %reshape.53 = f32[2,4,2,4,3,16,4]{6,5,4,3,2,1,0:T(8,128)S(1)} reshape(f32[8,8,192]{2,1,0:T(8,128)} %param.10) | data formatting | bytes 98304 | tf_op jit(solution)/shard_map/reshape | solution.py:551
  4.1 0.0 copy-start
  4.1 1.3 %copy.25 = f32[2,2,16,3,4,4,4]{2,1,0,6,5,4,3:T(2,128)S(1)} copy(f32[2,2,16,3,4,4,4]{6,2,3,5,1,4,0:T(8,128)S(1)} %bitcast.17) | data formatting | bytes 98304 | tf_op jit(solution)/shard_map/transpose | solution.py:551
  5.4 0.3 reshape.54
  5.7 0.7 copy.27.refs_0_
  6.4 0.0 copy-done
  6.4 0.8 reshape.55
  7.2 1.3 %copy.26 = f32[2,2,16,3,4,4,4]{2,1,0,6,5,4,3:T(2,128)S(1)} copy(f32[2,2,16,3,4,4,4]{6,2,3,5,1,4,0:T(8,128)S(1)} %bitcast.18) | data formatting | bytes 98304 | tf_op jit(solution)/shard_map/transpose | solution.py:551
  8.5 0.3 reshape.56
  8.9 0.7 copy.28.refs_1_
  9.6 80.3 %shard_map.177 = (f32[2560,256]{1,0:T(8,128)}, f32[64,256]{1,0:T(8,128)}) custom-call(f32[64,192]{1,0:T(8,128)} %copy.27.refs_0_, f32[64,192]{1,0:T(8,128)} %copy.28.refs_1_, f32[192,256]{1,0:T(8,128)} %refs_2_.1, f32[1,256]{1,0:T(1,128)} %bitcast.21, f32[256,768]{1,0:T(8,128)} %refs_4_.1, f32[256,256]{1,0:T(8,128)} %refs_5_.1, f32[1,256]{1,0:T(1,128)} %bitcast.22, ...), custom_call_target="tpu_custom_call" | custom-call | tf_op jit(solution)/shard_map/pallas_call | solution.py:540
  89.9 3.3 %shard_map.178 = (f32[1,1]{1,0:T(1,128)}, f32[64,256]{1,0:T(8,128)}, f32[192,256]{1,0:T(8,128)}, f32[1,256]{1,0:T(1,128)}, f32[256,768]{1,0:T(8,128)}, /*index=5...) custom-call(f32[2560,256]{1,0:T(8,128)} %get-tuple-element.22.packed, ...), custom_call_target="tpu_custom_call" | custom-call | tf_op jit(solution)/shard_map/pallas_call | solution.py:540
  93.2 0.9 copy.30
  94.2 1.7 %copy.32 = f32[256,192]{0,1:T(8,128)} copy(f32[256,192]{1,0:T(8,128)} %get-tuple-element.53) | data formatting | bytes 393216
  95.9 0.3 reshape.60
  96.3 1.2 %copy.31 = f32[2,4,2,4,3,16,4]{6,5,4,3,2,1,0:T(8,128)S(1)} copy(f32[2,4,2,4,3,16,4]{5,2,0,6,3,1,4:T(2,128)S(1)} %bitcast.19) | data formatting | bytes 98304 | tf_op jit(solution)/shard_map/transpose | solution.py:557
  97.5 1.3 %reshape.61 = f32[8,8,192]{2,1,0:T(8,128)} reshape(f32[2,4,2,4,3,16,4]{6,5,4,3,2,1,0:T(8,128)S(1)} %copy.31) | data formatting | bytes 98304 | tf_op jit(solution)/shard_map/reshape | solution.py:557
Async XLA Ops:
  4.1 2.4 %copy-start = (f32[8,8,192]{2,1,0:T(8,128)S(1)}, f32[8,8,192]{2,1,0:T(8,128)}, u32[]{:S(2)}) copy-start(f32[8,8,192]{2,1,0:T(8,128)} %param.11) | copy-start | bytes 147460
